TPU v7x, 256 devices: a whole 4x4x8 slice. The times are simulated.
256 devices in a mesh: rows: 64 (over y, z, core), groups: 4 (over x).
Axes of the slice: x: 4, y: 4, z: 8, core: 2. Of those that a mesh axis runs over, the one named last changes fastest.
Arguments:
- snapshots: bfloat16 [131072, 1024], P('rows', 'groups'), may hold values from -6 to 6
- mass_diag: float32 [131072], P('rows'), may hold values from 0.5 to 2
- lower_coupling: float32 [64, 128, 128], P('rows'), may hold values from -0.5 to 0.5
- upper_coupling: float32 [64, 128, 128], P('rows'), may hold values from -0.5 to 0.5
- band_offsets: int32 [64, 2], P('rows'), may hold values from 1 to 2
- start_basis: float32 [1024, 512], replicated, may hold values from -6 to 6
Outputs:
- modes: float32 [131072, 512], P('rows', 'groups')
All inputs are finite; a program needn't handle non-finite values.
Results may differ from a plain program's by a relative error of at most 0.0042.
Values may be sent and summed in bfloat16 or wider, within the bound.
No kernel may reach another device: no remote copies, remote signals or barrier semaphores. Data moves between devices by JAX's collectives and lax.ppermute only.
A program may use at most 128 MiB of HBM per device.

v0:
```python
import functools

import jax
import jax.numpy as jnp
from jax import lax
from jax.experimental import pallas as pl
from jax.experimental.pallas import tpu as pltpu
from jax.sharding import PartitionSpec as P

F32 = jnp.float32
BF16 = jnp.bfloat16
GROUPS = 4
BLOCK = 128
TILE = 8
WINDOW = 16
ROW_COL = ((1,), (0,))
ROW_ROW = ((1,), (1,))


def split(value):
    high = value.astype(BF16)
    return high, (value - high.astype(F32)).astype(BF16)


def dot3(left, right, dims):
    one = lambda a, b: lax.dot_general(a, b, (dims, ((), ())), preferred_element_type=F32)
    return one(left[0], right[0]) + (one(left[0], right[1]) + one(left[1], right[0]))


def row(tile, index):
    return jnp.broadcast_to(tile[index : index + 1], tile.shape)


def column(tile, index):
    return jnp.broadcast_to(tile[:, index : index + 1], tile.shape)


def total(terms):
    while len(terms) > 1:
        terms = [sum(terms[i : i + 2][1:], terms[i]) for i in range(0, len(terms), 2)]
    return terms[0]


def inverse_block(m, beside):
    n = m.shape[0]
    tiles = WINDOW // TILE
    lanes = lax.broadcasted_iota(jnp.int32, (1, n), 1)
    subs = lax.broadcasted_iota(jnp.int32, (TILE, n), 0)
    done = []
    near = [m[s * TILE : (s + 1) * TILE] for s in range(tiles)]
    rest = m[WINDOW:]
    for k in range(0, n, WINDOW):
        for _ in range(-(-len(beside) * WINDOW // (n - k))):
            beside.pop(0)()
        inside = (lanes >= k) & (lanes < k + WINDOW)
        cols = [[column(near[s], k + j) for j in range((s + 1) * TILE)] for s in range(tiles)]
        rows = [
            jnp.where(inside, jnp.where(lanes == subs + (k + s * TILE), 1.0, 0.0), near[s]) for s in range(tiles)
        ]
        entry, pivot_row, inverse = {}, {}, {}
        for a in range(0, WINDOW, 2):
            b, t = a + 1, a // TILE
            for p in (a, b):
                entry[p] = {j: row(cols[j // TILE][p], j % TILE) for j in range(p, WINDOW)}
                pivot_row[p] = row(rows[t], p % TILE)
            aa, ab, bb = entry[a][a], entry[a][b], entry[b][b]
            inverse[a] = 1.0 / (aa * bb - ab * ab)
            for s in range(t, tiles):
                if s == t and b % TILE == TILE - 1:
                    continue
                to_a = cols[s][a] * bb - cols[s][b] * ab
                to_b = cols[s][b] * aa - cols[s][a] * ab
                if s == t:
                    later = subs > b % TILE
                    to_a, to_b = jnp.where(later, to_a, 0.0), jnp.where(later, to_b, 0.0)
                for j in range(b + 1, (s + 1) * TILE):
                    cols[s][j] = cols[s][j] - (to_a * entry[a][j] + to_b * entry[b][j]) * inverse[a]
                rows[s] = rows[s] - (to_a * pivot_row[a] + to_b * pivot_row[b]) * inverse[a]
        for s in range(tiles):
            out = None
            for a in range(s * TILE, (s + 1) * TILE, 2):
                b = a + 1
                aa, ab, bb = entry[a][a], entry[a][b], entry[b][b]
                scale = lax.rsqrt(aa)
                first = pivot_row[a] * scale
                second = (pivot_row[b] * aa - pivot_row[a] * ab) * (scale * lax.rsqrt(aa * bb - ab * ab))
                out = first if out is None else jnp.where(subs == a % TILE, first, out)
                out = jnp.where(subs == b % TILE, second, out)
            done.append(out)
        if k + WINDOW == n:
            break
        solved = [None] * WINDOW
        for a in reversed(range(0, WINDOW, 2)):
            b = a + 1
            aa, ab, bb = entry[a][a], entry[a][b], entry[b][b]
            va, vb = pivot_row[a], pivot_row[b]
            for j in reversed(range(b + 1, WINDOW)):
                va, vb = va - entry[a][j] * solved[j], vb - entry[b][j] * solved[j]
            solved[a] = (bb * va - ab * vb) * inverse[a]
            solved[b] = (aa * vb - ab * va) * inverse[a]
        near = []
        for s in range(tiles):
            x = rest[s * TILE : (s + 1) * TILE]
            near.append(jnp.where(inside, 0.0, x) - total([column(x, k + j) * solved[j] for j in range(WINDOW)]))
        if k + 2 * WINDOW < n:
            x = rest[WINDOW:]
            pieces = [jnp.zeros((k, n), F32)] if k else []
            for s in range(tiles):
                tile = solved[s * TILE]
                for a in range(1, TILE):
                    tile = jnp.where(subs == a, solved[s * TILE + a], tile)
                pieces.append(tile)
            pieces.append(jnp.zeros((n - k - WINDOW, n), F32))
            rest = jnp.where(inside, 0.0, x) - dot3(split(x), split(jnp.concatenate(pieces, axis=0)), ROW_COL)
    r = lax.broadcasted_iota(jnp.int32, (n, n), 0)
    c = lax.broadcasted_iota(jnp.int32, (n, n), 1)
    return jnp.where(r >= c, jnp.concatenate(done, axis=0), 0.0)


def inverse_factor(m_ref, beside):
    n = m_ref.shape[0]
    tasks = []
    d = m_ref[:BLOCK, :BLOCK]
    for j, lo in enumerate(range(0, n, BLOCK)):
        hi = lo + BLOCK
        w = inverse_block(d, tasks + beside(j))
        ws = split(w)
        tasks = [functools.partial(finish_row, m_ref, lo, hi, w, ws)]
        if hi == n:
            break
        end = hi + BLOCK
        near = split(dot3(split(m_ref[hi:end, lo:hi]), ws, ROW_ROW))
        d = m_ref[hi:end, hi:end] - dot3(near, near, ROW_ROW)
        tasks += [functools.partial(finish_rows, m_ref, lo, hi, hi, end, near, None, ws)]
        if end < n:
            tasks += [functools.partial(finish_rows, m_ref, lo, hi, end, n, None, near, ws)]
    for task in tasks:
        task()


def equilibrate(m_ref, scale_ref):
    n = m_ref.shape[0]
    eye = lax.broadcasted_iota(jnp.int32, (BLOCK, BLOCK), 0) == lax.broadcasted_iota(jnp.int32, (BLOCK, BLOCK), 1)
    across = []
    for lo in range(0, n, BLOCK):
        hi = lo + BLOCK
        diagonal = jnp.where(eye, m_ref[lo:hi, lo:hi], 0.0)
        across.append(lax.rsqrt(jnp.sum(diagonal, axis=0, keepdims=True)))
        down = lax.rsqrt(jnp.sum(diagonal, axis=1, keepdims=True))
        scale_ref[:, lo:hi] = jnp.broadcast_to(across[-1], (TILE, BLOCK))
        for j, factor in enumerate(across):
            part = slice(j * BLOCK, (j + 1) * BLOCK)
            m_ref[lo:hi, part] = m_ref[lo:hi, part] * (down * factor)


def finish_row(m_ref, lo, hi, w, ws):
    if lo:
        m_ref[lo:hi, :lo] = dot3(ws, split(m_ref[lo:hi, :lo]), ROW_COL)
    m_ref[lo:hi, lo:hi] = w


def finish_rows(m_ref, lo, hi, start, end, factor, near, ws):
    if factor is None:
        factor = split(dot3(split(m_ref[start:end, lo:hi]), ws, ROW_ROW))
        m_ref[start:end, hi:start] = m_ref[start:end, hi:start] - dot3(factor, near, ROW_ROW)
        m_ref[start:end, start:end] = m_ref[start:end, start:end] - dot3(factor, factor, ROW_ROW)
    m_ref[start:end, lo:hi] = -dot3(factor, ws, ROW_COL)
    if lo:
        m_ref[start:end, :lo] = m_ref[start:end, :lo] - dot3(factor, split(m_ref[lo:hi, :lo]), ROW_COL)


def assemble(core, mine_ref, other_ref, gh_ref, gl_ref):
    size = gh_ref.shape[0] // GROUPS
    part = size // 2
    halves = ((mine_ref, core * part), (other_ref, (1 - core) * part))

    def place(value, row_at, col_at):
        where = pl.ds(pl.multiple_of(row_at, part), value.shape[0]), pl.ds(pl.multiple_of(col_at, part), value.shape[1])
        gh_ref[where], gl_ref[where] = split(value)

    for group in range(GROUPS):
        own, after = group * size, ((group + 1) % GROUPS) * size
        lo = group * 3 * size
        for ref, at in halves:
            place(ref[lo : lo + size, :], own, own + at)
            value = ref[lo + size : lo + 2 * size, :]
            place(value, after, own + at)
            place(value.T, own + at, after)
    for group in range(GROUPS // 2):
        after, last = (group + 1) * size, ((group - 1) % GROUPS) * size
        lo, opposite = (group * 3 + 2) * size, ((group + 2) * 3 + 2) * size
        for ref, at in halves:
            for ref_across, at_across in halves:
                value = ref[pl.ds(pl.multiple_of(lo + at_across, part), part), :]
                value = value + ref_across[pl.ds(pl.multiple_of(opposite + at, part), part), :].T
                place(value, after + at_across, last + at)
                place(value.T, last + at, after + at_across)


def iterate_kernel(
    iters, where_ref, mine_ref, other_ref, start_ref, out_ref, gh_ref, gl_ref, image_ref, ih_ref, il_ref, next_ref, m_ref, scale_ref
):
    assemble(where_ref[1], mine_ref, other_ref, gh_ref, gl_ref)
    n = m_ref.shape[0]
    half = n // 2
    image_ref[...] = dot3(split(start_ref[...]), (gh_ref[...], gl_ref[...]), ROW_COL)

    def orthonormalise(i, carry):
        @pl.when(i > 0)
        def _():
            high, low = split(next_ref[...])
            for lo in (0, half):
                hi = lo + half
                weights = split(lower(m_ref, lo, hi) * scale_ref[:1, :hi])
                image_ref[lo:hi, :] = dot3(weights, (high[:hi], low[:hi]), ROW_COL)

        ih_ref[...], il_ref[...] = split(image_ref[...])
        for lo in (0, half):
            left = (ih_ref[lo : lo + half], il_ref[lo : lo + half])
            for to in range(0, lo + 1, half):
                right = (ih_ref[to : to + half], il_ref[to : to + half])
                m_ref[lo : lo + half, to : to + half] = dot3(left, right, ROW_ROW)

        def part_of_next(rows, cols):
            left = (ih_ref[rows, :], il_ref[rows, :])
            next_ref[rows, cols] = dot3(left, (gh_ref[:, cols], gl_ref[:, cols]), ROW_COL)

        def beside(j):
            rows = pl.ds(j * BLOCK, BLOCK)
            width = 2 * BLOCK
            return [functools.partial(part_of_next, rows, pl.ds(at, width)) for at in range(0, gh_ref.shape[1], width)]

        equilibrate(m_ref, scale_ref)
        inverse_factor(m_ref, beside)
        return carry

    lax.fori_loop(0, iters, orthonormalise, 0)
    cols = n // GROUPS
    at = pl.multiple_of(where_ref[0] * cols, cols)
    r = lax.broadcasted_iota(jnp.int32, (cols, n), 0) + at
    c = lax.broadcasted_iota(jnp.int32, (cols, n), 1)
    weights = split(jnp.where(r >= c, m_ref[pl.ds(at, cols), :], 0.0) * scale_ref[:1, :])
    basis = dot3(weights, (ih_ref[...], il_ref[...]), ROW_COL).astype(BF16)
    next_ref[:cols, :] = basis.astype(F32)
    size = out_ref.shape[1] // GROUPS
    for q in range(GROUPS):
        source = pl.multiple_of(lax.rem(where_ref[0] + q, GROUPS) * size, size)
        out_ref[:, q * size : (q + 1) * size] = next_ref[:cols, pl.ds(source, size)].astype(BF16)


def lower(m_ref, lo, hi):
    r = lax.broadcasted_iota(jnp.int32, (hi - lo, hi), 0) + lo
    c = lax.broadcasted_iota(jnp.int32, (hi - lo, hi), 1)
    return jnp.where(r >= c, m_ref[lo:hi, :hi], 0.0)


def iterate(where, mine, other, start, iters):
    k, n = start.shape
    return pl.pallas_call(
        functools.partial(iterate_kernel, iters),
        out_shape=jax.ShapeDtypeStruct((k // GROUPS, n), BF16),
        in_specs=[pl.BlockSpec(memory_space=pltpu.SMEM)] + [pl.BlockSpec(memory_space=pltpu.VMEM)] * 3,
        out_specs=pl.BlockSpec(memory_space=pltpu.VMEM),
        scratch_shapes=[
            pltpu.VMEM((n, n), BF16),
            pltpu.VMEM((n, n), BF16),
            pltpu.VMEM((k, n), F32),
            pltpu.VMEM((k, n), BF16),
            pltpu.VMEM((k, n), BF16),
            pltpu.VMEM((k, n), F32),
            pltpu.VMEM((k, k), F32),
            pltpu.VMEM((TILE, k), F32),
        ],
        compiler_params=pltpu.CompilerParams(vmem_limit_bytes=30 * 2**20),
        cost_estimate=pl.CostEstimate(flops=10**6, bytes_accessed=2**20, transcendentals=0),
    )(where, mine, other, start)


def modes_kernel(h, *refs):
    *whole, basis_ref, out_ref = refs
    across = whole.pop()
    inner, rims = whole[:3], whole[3:]
    rows = out_ref.shape[0]
    middle = rows - 2 * h
    size = basis_ref.shape[1] // GROUPS

    def project(refs, lo, hi, at):
        result = None
        for q, value in enumerate((refs[0][lo:hi, :], refs[1][lo:hi, :], across[at + lo : at + hi, :], refs[2][lo:hi, :])):
            part = basis_ref[:, q * size : (q + 1) * size]
            term = lax.dot_general(value, part, (ROW_ROW, ((), ())), preferred_element_type=F32)
            result = term if result is None else result + term
        return result

    out_ref[:h, :] = project(rims, 0, h, middle)
    out_ref[rows - h :, :] = project(rims, h, 2 * h, middle)
    out_ref[h : rows - h, :] = project(inner, 0, middle, 0)


def modes(own, following, across, behind, basis, rows, h):
    parts = [[p[i] for p in (own, following, behind)] for i in (0, 1)]
    return pl.pallas_call(
        functools.partial(modes_kernel, h),
        out_shape=jax.ShapeDtypeStruct((rows, basis.shape[0]), F32),
        in_specs=[pl.BlockSpec(memory_space=pltpu.VMEM)] * 8,
        out_specs=pl.BlockSpec(memory_space=pltpu.VMEM),
        compiler_params=pltpu.CompilerParams(vmem_limit_bytes=16 * 2**20),
    )(*parts[0], *parts[1], across, basis)


ITERS = 3
ROWS = ("y", "z", "core")


def neighbour_rims(top, bottom, core):
    blocks = lax.axis_size(ROWS)
    h = top.shape[0]
    zero = core == 0
    sibling = turn(jnp.where(zero, top, bottom), "core", 1)
    both = jnp.where(zero, jnp.concatenate([bottom, sibling]), jnp.concatenate([sibling, top]))
    pairs = [(i, i + 2 - 4 * (i % 2)) for i in range(blocks) if 0 <= i + 2 - 4 * (i % 2) < blocks]
    far = lax.ppermute(both, ROWS, pairs)
    handed = jnp.where(zero, jnp.concatenate([bottom, far[h:]]), jnp.concatenate([top, far[:h]]))
    given = turn(handed, "core", 1)
    below = jnp.where(zero, jnp.concatenate([far[h:], far[:h]]), given)
    above = jnp.where(zero, given, far)
    return below, above


def turn(value, axis, by):
    size = lax.axis_size(axis)
    return lax.ppermute(value, axis, [(i, (i + by) % size) for i in range(size)])


def spread(value, axis):
    size = 1
    for name in axis if isinstance(axis, tuple) else (axis,):
        size *= lax.axis_size(name)
    copies = jnp.broadcast_to(value[None], (size,) + value.shape).reshape((size * value.shape[0],) + value.shape[1:])
    return lax.all_to_all(copies, axis, 0, 0, tiled=True)


def cross(left, right):
    return lax.dot_general(left, right, (((0,), (0,)), ((), ())), preferred_element_type=F32)


def rim(snaps, mass, coupling, rims, offset):
    h = snaps.shape[0]
    other = jnp.where(offset == 1, rims[:h], rims[h:]).astype(F32)
    terms = jnp.dot(coupling, other, precision=lax.Precision.HIGHEST, preferred_element_type=F32)
    return (mass[:, None] * snaps.astype(F32) + terms).astype(BF16)


def shards(snapshots, mass_diag, lower_coupling, upper_coupling, band_offsets, start_basis):
    block_rows, width = snapshots.shape
    h = lower_coupling.shape[1]
    total_rows = block_rows * lax.axis_size(ROWS)
    group = lax.axis_index("x")
    core = lax.axis_index("core")

    inner = (mass_diag[h : block_rows - h, None] * snapshots[h : block_rows - h].astype(F32)).astype(BF16)
    top, bottom = snapshots[:h], snapshots[block_rows - h :]
    below, above = neighbour_rims(top, bottom, core)
    rims = jnp.concatenate(
        [
            rim(top, mass_diag[:h], lower_coupling[0], below, band_offsets[0, 0]),
            rim(bottom, mass_diag[block_rows - h :], upper_coupling[0], above, band_offsets[0, 1]),
        ],
        axis=0,
    )

    late = (group >= GROUPS // 2).astype(jnp.int32)

    def halved(piece):
        part = piece.shape[0] // 2
        return lax.dynamic_slice_in_dim(piece, late * part, part, 0)

    own = [inner, rims]
    following = [turn(piece, "x", -1) for piece in own]
    behind = [turn(piece, "x", 1) for piece in own]
    blocks = [
        sum(cross(p, p) for p in own),
        sum(cross(f, p) for f, p in zip(following, own)),
        sum(cross(halved(f), halved(p)) for f, p in zip(following, behind)),
    ]
    partial = jnp.concatenate(blocks, axis=0)
    forward = jnp.concatenate(following, axis=0)
    partial, start = lax.optimization_barrier((partial, start_basis.T))
    lanes = width // 2
    keep = lax.dynamic_slice_in_dim(partial, core * lanes, lanes, 1)
    give = lax.dynamic_slice_in_dim(partial, (1 - core) * lanes, lanes, 1)
    chip = keep + turn(give, "core", 1)
    across = turn(forward, "x", -1)
    sources = lax.axis_size(("y", "z"))
    pieces = lax.all_to_all(chip, ("y", "z"), 0, 0, tiled=True)
    share = pieces.reshape((sources, -1, lanes)).sum(0) / total_rows
    halves = spread(spread(share, "z"), ("x", "y"))
    other_halves = turn(halves, "core", 1)

    where = jnp.stack([group, core]).astype(jnp.int32)
    basis = iterate(where, halves, other_halves, start, ITERS)
    return modes(own, following, across, behind, basis, block_rows, h)


def solution(mesh):
    fine = jax.sharding.Mesh(mesh.devices.reshape(4, 8, 2, 4), ("y", "z", "core", "x"))
    placed = (
        P(ROWS, "x"),
        P(ROWS),
        P(ROWS, None, None),
        P(ROWS, None, None),
        P(ROWS, None),
        P(),
    )
    return jax.shard_map(shards, mesh=fine, in_specs=placed, out_specs=P(ROWS, "x"), check_vma=False)
```

profile of v0, /device:TPU:1, one launch (start us, length us, event | category | flops | bytes accessed | tf_op | source)
XLA Modules:
  0.0 158.7 jit_solution(9056997906510362681)
XLA Ops:
  0.0 0.0 copy-start
  0.0 0.9 fusion.21
  0.9 3.3 %collective-permute-start.2 = (bf16[128,256]{1,0:T(8,128)(2,1)S(1)}, bf16[128,256]{1,0:T(8,128)(2,1)S(1)}, u32[]{:S(2)}, u32[]{:S(2)}) collective-permute-start(bf16[128,256]{1,0:T(8,128)(2,1)S(1)} %get-tuple-element.10), channel_id=1, source_target_pairs={{0,4},{4,0},{1,5},{5,1},{2,6},{6,2},{3,7},{7,3},{8,12},{12,8},{9,1... | collective-permute-start | bytes 196616 | tf_op jit(solution)/shard_map/ppermute | solution.py:332
  4.3 0.7 slice.44
  5.0 0.0 copy-start.3
  5.0 1.5 multiply_convert_fusion.refs_0_
  6.5 0.8 collective-permute-start
  7.3 0.7 collective-permute-start.1
  8.0 0.0 collective-permute-done.2
  8.0 1.3 collective-permute-start.3
  9.3 0.4 fusion.25
  9.8 0.0 copy-done.3
  9.8 0.6 fusion.24
  11.6 0.0 copy-start.4
  11.6 2.9 %copy.7 = f32[1024,512]{0,1:T(8,128)} copy(f32[1024,512]{1,0:T(8,128)} %param.11) | data formatting | bytes 4194304 | tf_op args[5]
  14.6 0.0 collective-permute-done.3
  14.6 2.2 %collective-permute-start.4 = (bf16[256,256]{1,0:T(8,128)(2,1)S(1)}, bf16[256,256]{1,0:T(8,128)(2,1)S(1)}, u32[]{:S(2)}, u32[]{:S(2)}) collective-permute-start(bf16[256,256]{1,0:T(8,128)(2,1)S(1)} %fusion.7), channel_id=1, source_target_pairs={{0,4},{4,0},{1,5},{5,1},{2,6},{6,2},{3,7},{7,3},{8,12},{12,8},{9,1... | collective-permute-start | bytes 393224 | tf_op jit(solution)/shard_map/ppermute | solution.py:332
  16.8 0.7 fusion.23
  17.5 0.3 collective-permute-done.4
  17.8 0.1 fusion.6
  17.9 0.0 copy-done
  17.9 1.0 fusion.2
  18.9 0.0 copy-done.4
  18.9 1.1 fusion.3
  20.0 3.0 %collective-permute-start.5 = (bf16[256,256]{1,0:T(8,128)(2,1)S(1)}, bf16[256,256]{1,0:T(8,128)(2,1)S(1)}, u32[]{:S(2)}, u32[]{:S(2)}) collective-permute-start(bf16[256,256]{1,0:T(8,128)(2,1)S(1)} %pad_maximum_fusion.6.refs_3_), channel_id=1, source_target_pairs={{0,3},{1,0},{2,1},{3,2},{4,7},{5,4},{6,5},{7,6},{8,11},{9,8},{10,9... | collective-permute-start | bytes 393224 | tf_op jit(solution)/shard_map/ppermute | solution.py:332
  23.0 0.0 collective-permute-start.6
  23.1 0.2 convolution_add_fusion.1
  23.3 8.0 %collective-permute-done.5.refs_4_ = bf16[256,256]{1,0:T(8,128)(2,1)S(1)} collective-permute-done((bf16[256,256]{1,0:T(8,128)(2,1)S(1)}, bf16[256,256]{1,0:T(8,128)(2,1)S(1)}, u32[]{:S(2)}, u32[]{:S(2)}) %collective-permute-start.5) | collective-permute-done | bytes 131104 | tf_op jit(solution)/shard_map/ppermute | solution.py:332
  31.3 1.6 %collective-permute-done.6.refs_5_ = bf16[256,256]{1,0:T(8,128)(2,1)S(1)} collective-permute-done((bf16[256,256]{1,0:T(8,128)(2,1)S(1)}, bf16[256,256]{1,0:T(8,128)(2,1)S(1)}, u32[]{:S(2)}, u32[]{:S(2)}) %collective-permute-start.6) | collective-permute-done | bytes 131104 | tf_op jit(solution)/shard_map/ppermute | solution.py:332
  32.9 0.2 fusion.13
  33.2 0.2 fusion.20
  33.4 0.0 collective-permute-done.refs_1_
  33.4 0.4 convolution_add_fusion
  33.8 0.0 collective-permute-done.1.refs_2_
  33.9 0.3 convolution_add_fusion.2
  34.2 0.1 pad_maximum_fusion.1
  34.3 0.0 copy-start.2
  34.3 0.9 copy-done.2
  35.2 0.8 constant_dynamic-slice_fusion
  35.9 1.1 collective-permute-start.8
  37.0 1.7 %collective-permute-done.8 = f32[768,128]{1,0:T(8,128)} collective-permute-done((f32[768,128]{1,0:T(8,128)}, f32[768,128]{1,0:T(8,128)}, u32[]{:S(2)}, u32[]{:S(2)}) %collective-permute-start.8) | collective-permute-done | bytes 393248 | tf_op jit(solution)/shard_map/ppermute | solution.py:332
  38.7 1.2 dynamic-slice_add_fusion
  39.9 22.9 %all_to_all.23 = f32[32,24,128]{2,1,0:T(8,128)} all-to-all(f32[32,24,128]{2,1,0:T(8,128)S(1)} %bitcast.34), channel_id=1, replica_groups=mesh['y'=4,'z'=8,'core'=2,'x'=4] {'y','z'}, dimensions={0} | all-to-all | bytes 786432 | tf_op jit(solution)/shard_map/all_to_all | solution.py:395
  62.8 1.0 reduce_sum.9
  63.8 13.0 %all_to_all.24 = f32[8,24,128]{2,1,0:T(8,128)S(1)} all-to-all(f32[8,24,128]{2,1,0:T(8,128)S(1)} %broadcast_in_dim.6), channel_id=1, replica_groups=mesh['y'=4,'z'=8,'core'=2,'x'=4] {'z'}, dimensions={0} | all-to-all | bytes 196608 | tf_op jit(solution)/shard_map/all_to_all | solution.py:340
  76.9 0.1 broadcast_in_dim.8
  77.0 22.0 %all_to_all.25 = f32[16,192,128]{2,1,0:T(8,128)S(1)} all-to-all(f32[16,192,128]{2,1,0:T(8,128)S(1)} %broadcast_in_dim.8), channel_id=1, replica_groups=mesh['y'=4,'z'=8,'core'=2,'x'=4] {'x','y'}, dimensions={0} | all-to-all | bytes 3145728 | tf_op jit(solution)/shard_map/all_to_all | solution.py:340
  99.0 0.0 copy-start.1
  99.0 4.7 %collective-permute-start.9 = (f32[3072,128]{1,0:T(8,128)S(1)}, f32[3072,128]{1,0:T(8,128)S(1)}, u32[]{:S(2)}, u32[]{:S(2)}) collective-permute-start(f32[3072,128]{1,0:T(8,128)S(1)} %bitcast.32), channel_id=1, source_target_pairs={{0,4},{4,0},{1,5},{5,1},{2,6},{6,2},{3,7},{7,3},{8,12},{12,8},{9,1... | collective-permute-start | bytes 4718600 | tf_op jit(solution)/shard_map/ppermute | solution.py:332
  103.7 0.1 pad_maximum_fusion
  103.8 1.1 collective-permute-start.7
  104.9 0.1 pad_add_fusion.where_ref
  104.9 1.8 %collective-permute-done.9.other_ref = f32[3072,128]{1,0:T(8,128)S(1)} collective-permute-done((f32[3072,128]{1,0:T(8,128)S(1)}, f32[3072,128]{1,0:T(8,128)S(1)}, u32[]{:S(2)}, u32[]{:S(2)}) %collective-permute-start.9) | collective-permute-done | bytes 1572896 | tf_op jit(solution)/shard_map/ppermute | solution.py:332
  106.7 0.0 copy-done.1
  106.8 49.7 %shard_map.64.refs_7_ = bf16[128,1024]{1,0:T(8,128)(2,1)S(1)} custom-call(s32[2]{0:T(128)S(1)} %pad_add_fusion.where_ref, f32[3072,128]{1,0:T(8,128)S(1)} %bitcast.33, f32[3072,128]{1,0:T(8,128)S(1)} %collective-permute-done.9.other_ref, f32[512,1024]{1,0:T(8,128)S(1)} %bitcast.31), custom_call_target="tpu_custom_call" | custom-call | flops 1000000 | bytes 1048576 | tf_op jit(solution)/shard_map/pallas_call | solution.py:259
  156.4 0.0 collective-permute-done.7.refs_6_
  156.4 2.2 %shard_map.65 = f32[2048,128]{1,0:T(8,128)} custom-call(bf16[1792,256]{1,0:T(8,128)(2,1)S(1)} %multiply_convert_fusion.refs_0_, bf16[1792,256]{1,0:T(8,128)(2,1)S(1)} %collective-permute-done.refs_1_, bf16[1792,256]{1,0:T(8,128)(2,1)S(1)} %collective-permute-done.1.refs_2_, bf16[256,256]{1,0:T(8,128)(2,1)S(1)} %pad_maximum_fusion.6.refs_3_, ...), custom_call_target="tpu_custom_call" | custom-call | tf_op jit(solution)/shard_map/pallas_call | solution.py:302
  (6 shorter events, 0.1 us)
Async XLA Ops:
  0.0 17.9 %copy-start = (f32[1,128,128]{2,1,0:T(8,128)S(1)}, f32[1,128,128]{2,1,0:T(8,128)}, u32[]{:S(2)}) copy-start(f32[1,128,128]{2,1,0:T(8,128)} %param.8) | copy-start | bytes 196612
  0.9 7.1 %collective-permute-start.2 = (bf16[128,256]{1,0:T(8,128)(2,1)S(1)}, bf16[128,256]{1,0:T(8,128)(2,1)S(1)}, u32[]{:S(2)}, u32[]{:S(2)}) collective-permute-start(bf16[128,256]{1,0:T(8,128)(2,1)S(1)} %get-tuple-element.10), channel_id=1, source_target_pairs={{0,4},{4,0},{1,5},{5,1},{2,6},{6,2},{3,7},{7,3},{8,12},{12,8},{9,1... | collective-permute-start | bytes 196616 | tf_op jit(solution)/shard_map/ppermute | solution.py:332
  5.0 4.8 %copy-start.3 = (s32[1,2]{1,0:T(1,128)S(1)}, s32[1,2]{1,0:T(1,128)}, u32[]{:S(2)}) copy-start(s32[1,2]{1,0:T(1,128)} %param.10) | copy-start | bytes 28
  6.5 26.9 %collective-permute-start = (bf16[1792,256]{1,0:T(8,128)(2,1)S(1)}, bf16[1792,256]{1,0:T(8,128)(2,1)S(1)}, u32[]{:S(2)}, u32[]{:S(2)}) collective-permute-start(bf16[1792,256]{1,0:T(8,128)(2,1)S(1)} %multiply_convert_fusion.refs_0_), channel_id=1, source_target_pairs={{0,3},{1,0},{2,1},{3,2},{4,7},{5,4},{6,5},{7,6},{8,11},{9,8},{10,9... | collective-permute-start | bytes 2752520 | tf_op jit(solution)/shard_map/ppermute | solution.py:332
  7.3 26.6 %collective-permute-start.1 = (bf16[1792,256]{1,0:T(8,128)(2,1)S(1)}, bf16[1792,256]{1,0:T(8,128)(2,1)S(1)}, u32[]{:S(2)}, u32[]{:S(2)}) collective-permute-start(bf16[1792,256]{1,0:T(8,128)(2,1)S(1)} %multiply_convert_fusion.refs_0_), channel_id=1, source_target_pairs={{0,1},{1,2},{2,3},{3,0},{4,5},{5,6},{6,7},{7,4},{8,9},{9,10},{10,1... | collective-permute-start | bytes 2752520 | tf_op jit(solution)/shard_map/ppermute | solution.py:332
  8.0 6.5 %collective-permute-start.3 = (bf16[256,256]{1,0:T(8,128)(2,1)S(1)}, bf16[256,256]{1,0:T(8,128)(2,1)S(1)}, u32[]{:S(2)}, u32[]{:S(2)}) collective-permute-start(bf16[256,256]{1,0:T(8,128)(2,1)S(1)} %fusion.8), channel_id=1, source_target_pairs={{0,8},{8,16},{12,4},{16,24},{20,12},{24,32},{28,20},{32,40},{36,28... | collective-permute-start | bytes 393224 | tf_op jit(solution)/shard_map/ppermute | solution.py:322
  11.6 7.3 %copy-start.4 = (f32[1,128,128]{2,1,0:T(8,128)S(1)}, f32[1,128,128]{2,1,0:T(8,128)}, u32[]{:S(2)}) copy-start(f32[1,128,128]{2,1,0:T(8,128)} %param.9) | copy-start | bytes 196612
  14.6 3.2 %collective-permute-start.4 = (bf16[256,256]{1,0:T(8,128)(2,1)S(1)}, bf16[256,256]{1,0:T(8,128)(2,1)S(1)}, u32[]{:S(2)}, u32[]{:S(2)}) collective-permute-start(bf16[256,256]{1,0:T(8,128)(2,1)S(1)} %fusion.7), channel_id=1, source_target_pairs={{0,4},{4,0},{1,5},{5,1},{2,6},{6,2},{3,7},{7,3},{8,12},{12,8},{9,1... | collective-permute-start | bytes 393224 | tf_op jit(solution)/shard_map/ppermute | solution.py:332
  20.0 11.3 %collective-permute-start.5 = (bf16[256,256]{1,0:T(8,128)(2,1)S(1)}, bf16[256,256]{1,0:T(8,128)(2,1)S(1)}, u32[]{:S(2)}, u32[]{:S(2)}) collective-permute-start(bf16[256,256]{1,0:T(8,128)(2,1)S(1)} %pad_maximum_fusion.6.refs_3_), channel_id=1, source_target_pairs={{0,3},{1,0},{2,1},{3,2},{4,7},{5,4},{6,5},{7,6},{8,11},{9,8},{10,9... | collective-permute-start | bytes 393224 | tf_op jit(solution)/shard_map/ppermute | solution.py:332
  23.0 9.9 %collective-permute-start.6 = (bf16[256,256]{1,0:T(8,128)(2,1)S(1)}, bf16[256,256]{1,0:T(8,128)(2,1)S(1)}, u32[]{:S(2)}, u32[]{:S(2)}) collective-permute-start(bf16[256,256]{1,0:T(8,128)(2,1)S(1)} %pad_maximum_fusion.6.refs_3_), channel_id=1, source_target_pairs={{0,1},{1,2},{2,3},{3,0},{4,5},{5,6},{6,7},{7,4},{8,9},{9,10},{10,1... | collective-permute-start | bytes 393224 | tf_op jit(solution)/shard_map/ppermute | solution.py:332
  34.3 0.9 copy-start.2
  35.9 2.8 %collective-permute-start.8 = (f32[768,128]{1,0:T(8,128)}, f32[768,128]{1,0:T(8,128)}, u32[]{:S(2)}, u32[]{:S(2)}) collective-permute-start(f32[768,128]{1,0:T(8,128)} %constant_dynamic-slice_fusion), channel_id=1, source_target_pairs={{0,4},{4,0},{1,5},{5,1},{2,6},{6,2},{3,7},{7,3},{8,12},{12,8},{9,1... | collective-permute-start | bytes 1179656 | tf_op jit(solution)/shard_map/ppermute | solution.py:332
  99.0 7.7 %copy-start.1 = (f32[1024,512]{0,1:T(8,128)S(1)}, f32[1024,512]{0,1:T(8,128)}, u32[]{:S(2)}) copy-start(f32[1024,512]{0,1:T(8,128)} %copy.7) | copy-start | bytes 6291460
  99.0 7.7 %collective-permute-start.9 = (f32[3072,128]{1,0:T(8,128)S(1)}, f32[3072,128]{1,0:T(8,128)S(1)}, u32[]{:S(2)}, u32[]{:S(2)}) collective-permute-start(f32[3072,128]{1,0:T(8,128)S(1)} %bitcast.32), channel_id=1, source_target_pairs={{0,4},{4,0},{1,5},{5,1},{2,6},{6,2},{3,7},{7,3},{8,12},{12,8},{9,1... | collective-permute-start | bytes 4718600 | tf_op jit(solution)/shard_map/ppermute | solution.py:332
  103.8 52.6 %collective-permute-start.7 = (bf16[2048,256]{1,0:T(8,128)(2,1)S(1)}, bf16[2048,256]{1,0:T(8,128)(2,1)S(1)}, u32[]{:S(2)}, u32[]{:S(2)}) collective-permute-start(bf16[2048,256]{1,0:T(8,128)(2,1)S(1)} %pad_maximum_fusion), channel_id=1, source_target_pairs={{0,3},{1,0},{2,1},{3,2},{4,7},{5,4},{6,5},{7,6},{8,11},{9,8},{10,9... | collective-permute-start | bytes 3145736 | tf_op jit(solution)/shard_map/ppermute | solution.py:332
where the time goes:
time: 159 us
  blocking collectives  57.9 us (36%)
  Pallas kernels  51.9 us (33%)
  starting transfers between devices  18.3 us (12%)
  waiting for transfers between devices  13.5 us (8%)
  local copies, waits for them, and re-layouts  6.75 us (4%)
  other arithmetic  4.94 us (3%)
  matrix products  3.97 us (2%)
    pallas_call x1, Pallas kernels, iterate(): pl.pallas_call(functools.partial(iterate_kernel, iters), out_shape=jax.Sh...  49.7 us
    all_to_all x2, blocking collectives, spread(): return lax.all_to_all(copies, axis, 0, 0, tiled=True)  35 us
    all_to_all x1, blocking collectives, shards(): pieces = lax.all_to_all(chip, ('y', 'z'), 0, 0, tiled=True)  22.9 us
    ppermute x9, starting transfers between devices, turn(): lax.ppermute(value, axis, [(i, (i + by) % size) for i in range(size)])  17 us
    ppermute x9, waiting for transfers between devices, turn(): lax.ppermute(value, axis, [(i, (i + by) % size) for i in range(size)])  13.4 us
    unnamed x11, local copies, waits for them, and re-layouts  3.84 us
  transfers between devices with their start and end apart: 10, of which 5 were waited for; matrix products, arithmetic and copies ran while one was open for 7% of the time, Pallas kernels for 31%

commit v1 on v0

--- a/solution.py
+++ b/solution.py
@@ -359,7 +359,7 @@
     core = lax.axis_index("core")
 
     inner = (mass_diag[h : block_rows - h, None] * snapshots[h : block_rows - h].astype(F32)).astype(BF16)
-    top, bottom = snapshots[:h], snapshots[block_rows - h :]
+    inner, top, bottom = lax.optimization_barrier((inner, snapshots[:h], snapshots[block_rows - h :]))
     below, above = neighbour_rims(top, bottom, core)
     rims = jnp.concatenate(
         [
@@ -387,8 +387,8 @@
     forward = jnp.concatenate(following, axis=0)
     partial, start = lax.optimization_barrier((partial, start_basis.T))
     lanes = width // 2
-    keep = lax.dynamic_slice_in_dim(partial, core * lanes, lanes, 1)
-    give = lax.dynamic_slice_in_dim(partial, (1 - core) * lanes, lanes, 1)
+    keep = jnp.where(core == 0, partial[:, :lanes], partial[:, lanes:])
+    give = jnp.where(core == 0, partial[:, lanes:], partial[:, :lanes])
     chip = keep + turn(give, "core", 1)
     across = turn(forward, "x", -1)
     sources = lax.axis_size(("y", "z"))

time: 159 us -> 156 us (0.981)
  other arithmetic: 4.94 us -> 3 us
  matrix products: 3.97 us -> 2.29 us
    dot_general x2, matrix products: 2.1 us -> 0.42 us  [rim(): jnp.dot(coupling, other, precision=lax.Precision.HIGHEST, preferred_eleme...]
    unnamed x11 -> x9, local copies, waits for them, and re-layouts: 3.84 us -> 2.95 us
  transfers between devices with their start and end apart: 10 -> 10, of which waited for: 5 -> 5; matrix products, arithmetic and copies ran while one was open for 7% -> 4% of each run, Pallas kernels for 31% -> 32%
where the time goes in v1:
time: 156 us
  blocking collectives  57.9 us (37%)
  Pallas kernels  51.9 us (33%)
  starting transfers between devices  18.4 us (12%)
  waiting for transfers between devices  14.7 us (9%)
  local copies, waits for them, and re-layouts  6.04 us (4%)
  other arithmetic  3 us (2%)
  matrix products  2.29 us (1%)
    pallas_call x1, Pallas kernels, iterate(): pl.pallas_call(functools.partial(iterate_kernel, iters), out_shape=jax.Sh...  49.6 us
    all_to_all x2, blocking collectives, spread(): return lax.all_to_all(copies, axis, 0, 0, tiled=True)  35 us
    all_to_all x1, blocking collectives, shards(): pieces = lax.all_to_all(chip, ('y', 'z'), 0, 0, tiled=True)  22.9 us
    ppermute x9, starting transfers between devices, turn(): lax.ppermute(value, axis, [(i, (i + by) % size) for i in range(size)])  17.2 us
    ppermute x9, waiting for transfers between devices, turn(): lax.ppermute(value, axis, [(i, (i + by) % size) for i in range(size)])  14.7 us
  transfers between devices with their start and end apart: 10, of which 5 were waited for; matrix products, arithmetic and copies ran while one was open for 4% of the time, Pallas kernels for 32%

profile of v1, /device:TPU:1, one launch (start us, length us, event | category | flops | bytes accessed | tf_op | source)
XLA Modules:
  0.0 155.7 jit_solution(17219743360999496950)
XLA Ops:
  0.0 0.0 copy-start
  0.0 0.9 fusion.21
  0.9 0.7 slice.52
  1.6 0.0 copy-start.2
  1.6 1.5 multiply_convert_fusion.refs_0_
  3.1 3.3 %collective-permute-start.2 = (bf16[128,256]{1,0:T(8,128)(2,1)S(1)}, bf16[128,256]{1,0:T(8,128)(2,1)S(1)}, u32[]{:S(2)}, u32[]{:S(2)}) collective-permute-start(bf16[128,256]{1,0:T(8,128)(2,1)S(1)} %broadcast_select_fusion.1), channel_id=1, source_target_pairs={{0,4},{4,0},{1,5},{5,1},{2,6},{6,2},{3,7},{7,3},{8,12},{12,8},{9,1... | collective-permute-start | bytes 196616 | tf_op jit(solution)/shard_map/ppermute | solution.py:332
  6.5 0.8 collective-permute-start
  7.2 0.7 collective-permute-start.1
  8.0 0.0 collective-permute-done.2
  8.0 1.3 collective-permute-start.3
  9.3 0.4 fusion.25
  9.7 0.0 copy-done.2
  9.8 0.6 fusion.24
  11.6 0.0 copy-start.3
  11.6 2.9 %copy.7 = f32[1024,512]{0,1:T(8,128)} copy(f32[1024,512]{1,0:T(8,128)} %param.11) | data formatting | bytes 4194304 | tf_op args[5]
  14.5 0.0 collective-permute-done.3
  14.6 2.3 %collective-permute-start.4 = (bf16[256,256]{1,0:T(8,128)(2,1)S(1)}, bf16[256,256]{1,0:T(8,128)(2,1)S(1)}, u32[]{:S(2)}, u32[]{:S(2)}) collective-permute-start(bf16[256,256]{1,0:T(8,128)(2,1)S(1)} %fusion.7), channel_id=1, source_target_pairs={{0,4},{4,0},{1,5},{5,1},{2,6},{6,2},{3,7},{7,3},{8,12},{12,8},{9,1... | collective-permute-start | bytes 393224 | tf_op jit(solution)/shard_map/ppermute | solution.py:332
  16.8 0.7 fusion.23
  17.5 0.3 collective-permute-done.4
  17.8 0.1 fusion.6
  17.9 0.0 copy-done
  17.9 0.2 fusion.2
  18.1 0.0 copy-done.3
  18.1 0.2 fusion.3
  18.3 3.0 %collective-permute-start.5 = (bf16[256,256]{1,0:T(8,128)(2,1)S(1)}, bf16[256,256]{1,0:T(8,128)(2,1)S(1)}, u32[]{:S(2)}, u32[]{:S(2)}) collective-permute-start(bf16[256,256]{1,0:T(8,128)(2,1)S(1)} %pad_maximum_fusion.6.refs_3_), channel_id=1, source_target_pairs={{0,3},{1,0},{2,1},{3,2},{4,7},{5,4},{6,5},{7,6},{8,11},{9,8},{10,9... | collective-permute-start | bytes 393224 | tf_op jit(solution)/shard_map/ppermute | solution.py:332
  21.4 0.0 collective-permute-start.6
  21.4 0.2 convolution_add_fusion.1
  21.6 9.6 %collective-permute-done.5.refs_4_ = bf16[256,256]{1,0:T(8,128)(2,1)S(1)} collective-permute-done((bf16[256,256]{1,0:T(8,128)(2,1)S(1)}, bf16[256,256]{1,0:T(8,128)(2,1)S(1)}, u32[]{:S(2)}, u32[]{:S(2)}) %collective-permute-start.5) | collective-permute-done | bytes 131104 | tf_op jit(solution)/shard_map/ppermute | solution.py:332
  31.2 1.6 %collective-permute-done.6.refs_5_ = bf16[256,256]{1,0:T(8,128)(2,1)S(1)} collective-permute-done((bf16[256,256]{1,0:T(8,128)(2,1)S(1)}, bf16[256,256]{1,0:T(8,128)(2,1)S(1)}, u32[]{:S(2)}, u32[]{:S(2)}) %collective-permute-start.6) | collective-permute-done | bytes 131104 | tf_op jit(solution)/shard_map/ppermute | solution.py:332
  32.8 0.2 fusion.13
  33.0 0.2 fusion.20
  33.3 0.0 collective-permute-done.refs_1_
  33.3 0.4 convolution_add_fusion
  33.7 0.0 collective-permute-done.1.refs_2_
  33.7 0.3 convolution_add_fusion.2
  34.1 0.1 pad_maximum_fusion.1
  34.2 1.3 collective-permute-start.8
  35.5 1.3 collective-permute-done.8
  36.8 0.1 select_add_fusion
  36.9 22.9 %all_to_all.23 = f32[32,24,128]{2,1,0:T(8,128)} all-to-all(f32[32,24,128]{2,1,0:T(8,128)S(1)} %bitcast.34), channel_id=1, replica_groups=mesh['y'=4,'z'=8,'core'=2,'x'=4] {'y','z'}, dimensions={0} | all-to-all | bytes 786432 | tf_op jit(solution)/shard_map/all_to_all | solution.py:395
  59.8 1.0 reduce_sum.9
  60.9 13.0 %all_to_all.24 = f32[8,24,128]{2,1,0:T(8,128)S(1)} all-to-all(f32[8,24,128]{2,1,0:T(8,128)S(1)} %broadcast_in_dim.6), channel_id=1, replica_groups=mesh['y'=4,'z'=8,'core'=2,'x'=4] {'z'}, dimensions={0} | all-to-all | bytes 196608 | tf_op jit(solution)/shard_map/all_to_all | solution.py:340
  73.9 0.1 broadcast_in_dim.8
  74.1 22.0 %all_to_all.25 = f32[16,192,128]{2,1,0:T(8,128)S(1)} all-to-all(f32[16,192,128]{2,1,0:T(8,128)S(1)} %broadcast_in_dim.8), channel_id=1, replica_groups=mesh['y'=4,'z'=8,'core'=2,'x'=4] {'x','y'}, dimensions={0} | all-to-all | bytes 3145728 | tf_op jit(solution)/shard_map/all_to_all | solution.py:340
  96.0 0.0 copy-start.1
  96.0 4.7 %collective-permute-start.9 = (f32[3072,128]{1,0:T(8,128)S(1)}, f32[3072,128]{1,0:T(8,128)S(1)}, u32[]{:S(2)}, u32[]{:S(2)}) collective-permute-start(f32[3072,128]{1,0:T(8,128)S(1)} %bitcast.32), channel_id=1, source_target_pairs={{0,4},{4,0},{1,5},{5,1},{2,6},{6,2},{3,7},{7,3},{8,12},{12,8},{9,1... | collective-permute-start | bytes 4718600 | tf_op jit(solution)/shard_map/ppermute | solution.py:332
  100.7 0.1 pad_maximum_fusion
  100.8 1.1 collective-permute-start.7
  101.9 0.1 pad_add_fusion.where_ref
  102.0 1.8 %collective-permute-done.9.other_ref = f32[3072,128]{1,0:T(8,128)S(1)} collective-permute-done((f32[3072,128]{1,0:T(8,128)S(1)}, f32[3072,128]{1,0:T(8,128)S(1)}, u32[]{:S(2)}, u32[]{:S(2)}) %collective-permute-start.9) | collective-permute-done | bytes 1572896 | tf_op jit(solution)/shard_map/ppermute | solution.py:332
  103.8 0.0 copy-done.1
  103.8 49.6 %shard_map.64.refs_7_ = bf16[128,1024]{1,0:T(8,128)(2,1)S(1)} custom-call(s32[2]{0:T(128)S(1)} %pad_add_fusion.where_ref, f32[3072,128]{1,0:T(8,128)S(1)} %bitcast.33, f32[3072,128]{1,0:T(8,128)S(1)} %collective-permute-done.9.other_ref, f32[512,1024]{1,0:T(8,128)S(1)} %bitcast.31), custom_call_target="tpu_custom_call" | custom-call | flops 1000000 | bytes 1048576 | tf_op jit(solution)/shard_map/pallas_call | solution.py:259
  153.4 0.0 collective-permute-done.7.refs_6_
  153.4 2.2 %shard_map.65 = f32[2048,128]{1,0:T(8,128)} custom-call(bf16[1792,256]{1,0:T(8,128)(2,1)S(1)} %multiply_convert_fusion.refs_0_, bf16[1792,256]{1,0:T(8,128)(2,1)S(1)} %collective-permute-done.refs_1_, bf16[1792,256]{1,0:T(8,128)(2,1)S(1)} %collective-permute-done.1.refs_2_, bf16[256,256]{1,0:T(8,128)(2,1)S(1)} %pad_maximum_fusion.6.refs_3_, ...), custom_call_target="tpu_custom_call" | custom-call | tf_op jit(solution)/shard_map/pallas_call | solution.py:302
  (8 shorter events, 0.2 us)
Async XLA Ops:
  0.0 17.9 %copy-start = (f32[1,128,128]{2,1,0:T(8,128)S(1)}, f32[1,128,128]{2,1,0:T(8,128)}, u32[]{:S(2)}) copy-start(f32[1,128,128]{2,1,0:T(8,128)} %param.8) | copy-start | bytes 196612
  1.6 8.1 %copy-start.2 = (s32[1,2]{1,0:T(1,128)S(1)}, s32[1,2]{1,0:T(1,128)}, u32[]{:S(2)}) copy-start(s32[1,2]{1,0:T(1,128)} %param.10) | copy-start | bytes 28
  3.1 4.8 %collective-permute-start.2 = (bf16[128,256]{1,0:T(8,128)(2,1)S(1)}, bf16[128,256]{1,0:T(8,128)(2,1)S(1)}, u32[]{:S(2)}, u32[]{:S(2)}) collective-permute-start(bf16[128,256]{1,0:T(8,128)(2,1)S(1)} %broadcast_select_fusion.1), channel_id=1, source_target_pairs={{0,4},{4,0},{1,5},{5,1},{2,6},{6,2},{3,7},{7,3},{8,12},{12,8},{9,1... | collective-permute-start | bytes 196616 | tf_op jit(solution)/shard_map/ppermute | solution.py:332
  6.5 26.8 %collective-permute-start = (bf16[1792,256]{1,0:T(8,128)(2,1)S(1)}, bf16[1792,256]{1,0:T(8,128)(2,1)S(1)}, u32[]{:S(2)}, u32[]{:S(2)}) collective-permute-start(bf16[1792,256]{1,0:T(8,128)(2,1)S(1)} %multiply_convert_fusion.refs_0_), channel_id=1, source_target_pairs={{0,3},{1,0},{2,1},{3,2},{4,7},{5,4},{6,5},{7,6},{8,11},{9,8},{10,9... | collective-permute-start | bytes 2752520 | tf_op jit(solution)/shard_map/ppermute | solution.py:332
  7.2 26.5 %collective-permute-start.1 = (bf16[1792,256]{1,0:T(8,128)(2,1)S(1)}, bf16[1792,256]{1,0:T(8,128)(2,1)S(1)}, u32[]{:S(2)}, u32[]{:S(2)}) collective-permute-start(bf16[1792,256]{1,0:T(8,128)(2,1)S(1)} %multiply_convert_fusion.refs_0_), channel_id=1, source_target_pairs={{0,1},{1,2},{2,3},{3,0},{4,5},{5,6},{6,7},{7,4},{8,9},{9,10},{10,1... | collective-permute-start | bytes 2752520 | tf_op jit(solution)/shard_map/ppermute | solution.py:332
  8.0 6.5 %collective-permute-start.3 = (bf16[256,256]{1,0:T(8,128)(2,1)S(1)}, bf16[256,256]{1,0:T(8,128)(2,1)S(1)}, u32[]{:S(2)}, u32[]{:S(2)}) collective-permute-start(bf16[256,256]{1,0:T(8,128)(2,1)S(1)} %fusion.8), channel_id=1, source_target_pairs={{0,8},{8,16},{12,4},{16,24},{20,12},{24,32},{28,20},{32,40},{36,28... | collective-permute-start | bytes 393224 | tf_op jit(solution)/shard_map/ppermute | solution.py:322
  11.6 6.5 %copy-start.3 = (f32[1,128,128]{2,1,0:T(8,128)S(1)}, f32[1,128,128]{2,1,0:T(8,128)}, u32[]{:S(2)}) copy-start(f32[1,128,128]{2,1,0:T(8,128)} %param.9) | copy-start | bytes 196612
  14.6 3.2 %collective-permute-start.4 = (bf16[256,256]{1,0:T(8,128)(2,1)S(1)}, bf16[256,256]{1,0:T(8,128)(2,1)S(1)}, u32[]{:S(2)}, u32[]{:S(2)}) collective-permute-start(bf16[256,256]{1,0:T(8,128)(2,1)S(1)} %fusion.7), channel_id=1, source_target_pairs={{0,4},{4,0},{1,5},{5,1},{2,6},{6,2},{3,7},{7,3},{8,12},{12,8},{9,1... | collective-permute-start | bytes 393224 | tf_op jit(solution)/shard_map/ppermute | solution.py:332
  18.3 12.9 %collective-permute-start.5 = (bf16[256,256]{1,0:T(8,128)(2,1)S(1)}, bf16[256,256]{1,0:T(8,128)(2,1)S(1)}, u32[]{:S(2)}, u32[]{:S(2)}) collective-permute-start(bf16[256,256]{1,0:T(8,128)(2,1)S(1)} %pad_maximum_fusion.6.refs_3_), channel_id=1, source_target_pairs={{0,3},{1,0},{2,1},{3,2},{4,7},{5,4},{6,5},{7,6},{8,11},{9,8},{10,9... | collective-permute-start | bytes 393224 | tf_op jit(solution)/shard_map/ppermute | solution.py:332
  21.4 11.5 %collective-permute-start.6 = (bf16[256,256]{1,0:T(8,128)(2,1)S(1)}, bf16[256,256]{1,0:T(8,128)(2,1)S(1)}, u32[]{:S(2)}, u32[]{:S(2)}) collective-permute-start(bf16[256,256]{1,0:T(8,128)(2,1)S(1)} %pad_maximum_fusion.6.refs_3_), channel_id=1, source_target_pairs={{0,1},{1,2},{2,3},{3,0},{4,5},{5,6},{6,7},{7,4},{8,9},{9,10},{10,1... | collective-permute-start | bytes 393224 | tf_op jit(solution)/shard_map/ppermute | solution.py:332
  34.2 2.6 %collective-permute-start.8 = (f32[768,128]{1,0:T(8,128)S(1)}, f32[768,128]{1,0:T(8,128)S(1)}, u32[]{:S(2)}, u32[]{:S(2)}) collective-permute-start(f32[768,128]{1,0:T(8,128)S(1)} %slice_select_fusion), channel_id=1, source_target_pairs={{0,4},{4,0},{1,5},{5,1},{2,6},{6,2},{3,7},{7,3},{8,12},{12,8},{9,1... | collective-permute-start | bytes 1179656 | tf_op jit(solution)/shard_map/ppermute | solution.py:332
  96.0 7.7 %copy-start.1 = (f32[1024,512]{0,1:T(8,128)S(1)}, f32[1024,512]{0,1:T(8,128)}, u32[]{:S(2)}) copy-start(f32[1024,512]{0,1:T(8,128)} %copy.7) | copy-start | bytes 6291460
  96.0 7.7 %collective-permute-start.9 = (f32[3072,128]{1,0:T(8,128)S(1)}, f32[3072,128]{1,0:T(8,128)S(1)}, u32[]{:S(2)}, u32[]{:S(2)}) collective-permute-start(f32[3072,128]{1,0:T(8,128)S(1)} %bitcast.32), channel_id=1, source_target_pairs={{0,4},{4,0},{1,5},{5,1},{2,6},{6,2},{3,7},{7,3},{8,12},{12,8},{9,1... | collective-permute-start | bytes 4718600 | tf_op jit(solution)/shard_map/ppermute | solution.py:332
  100.8 52.6 %collective-permute-start.7 = (bf16[2048,256]{1,0:T(8,128)(2,1)S(1)}, bf16[2048,256]{1,0:T(8,128)(2,1)S(1)}, u32[]{:S(2)}, u32[]{:S(2)}) collective-permute-start(bf16[2048,256]{1,0:T(8,128)(2,1)S(1)} %pad_maximum_fusion), channel_id=1, source_target_pairs={{0,3},{1,0},{2,1},{3,2},{4,7},{5,4},{6,5},{7,6},{8,11},{9,8},{10,9... | collective-permute-start | bytes 3145736 | tf_op jit(solution)/shard_map/ppermute | solution.py:332

commit v2 on v1

--- a/solution.py
+++ b/solution.py
@@ -271,7 +271,7 @@
             pltpu.VMEM((k, k), F32),
             pltpu.VMEM((TILE, k), F32),
         ],
-        compiler_params=pltpu.CompilerParams(vmem_limit_bytes=30 * 2**20),
+        compiler_params=pltpu.CompilerParams(vmem_limit_bytes=20 * 2**20),
         cost_estimate=pl.CostEstimate(flops=10**6, bytes_accessed=2**20, transcendentals=0),
     )(where, mine, other, start)
 

time: 156 us -> 156 us (level)
  no operation moved by 1% of the time
where the time goes in v2:
time: 156 us
  blocking collectives  57.9 us (37%)
  Pallas kernels  51.9 us (33%)
  starting transfers between devices  18.4 us (12%)
  waiting for transfers between devices  14.7 us (9%)
  local copies, waits for them, and re-layouts  6.04 us (4%)
  other arithmetic  3 us (2%)
  matrix products  2.29 us (1%)
    pallas_call x1, Pallas kernels, iterate(): pl.pallas_call(functools.partial(iterate_kernel, iters), out_shape=jax.Sh...  49.6 us
    all_to_all x2, blocking collectives, spread(): return lax.all_to_all(copies, axis, 0, 0, tiled=True)  35 us
    all_to_all x1, blocking collectives, shards(): pieces = lax.all_to_all(chip, ('y', 'z'), 0, 0, tiled=True)  22.9 us
    ppermute x9, starting transfers between devices, turn(): lax.ppermute(value, axis, [(i, (i + by) % size) for i in range(size)])  17.2 us
    ppermute x9, waiting for transfers between devices, turn(): lax.ppermute(value, axis, [(i, (i + by) % size) for i in range(size)])  14.7 us
  transfers between devices with their start and end apart: 10, of which 5 were waited for; matrix products, arithmetic and copies ran while one was open for 4% of the time, Pallas kernels for 32%

profile of v2, /device:TPU:1, one launch (start us, length us, event | category | flops | bytes accessed | tf_op | source)
XLA Modules:
  0.0 155.7 jit_solution(4123977283284519195)
XLA Ops:
  0.0 0.0 copy-start
  0.0 0.9 fusion.21
  0.9 0.7 slice.52
  1.6 0.0 copy-start.2
  1.6 1.5 multiply_convert_fusion.refs_0_
  3.1 3.3 %collective-permute-start.2 = (bf16[128,256]{1,0:T(8,128)(2,1)S(1)}, bf16[128,256]{1,0:T(8,128)(2,1)S(1)}, u32[]{:S(2)}, u32[]{:S(2)}) collective-permute-start(bf16[128,256]{1,0:T(8,128)(2,1)S(1)} %broadcast_select_fusion.1), channel_id=1, source_target_pairs={{0,4},{4,0},{1,5},{5,1},{2,6},{6,2},{3,7},{7,3},{8,12},{12,8},{9,1... | collective-permute-start | bytes 196616 | tf_op jit(solution)/shard_map/ppermute | solution.py:332
  6.5 0.8 collective-permute-start
  7.2 0.7 collective-permute-start.1
  8.0 0.0 collective-permute-done.2
  8.0 1.3 collective-permute-start.3
  9.3 0.4 fusion.25
  9.7 0.0 copy-done.2
  9.8 0.6 fusion.24
  11.6 0.0 copy-start.3
  11.6 2.9 %copy.7 = f32[1024,512]{0,1:T(8,128)} copy(f32[1024,512]{1,0:T(8,128)} %param.11) | data formatting | bytes 4194304 | tf_op args[5]
  14.5 0.0 collective-permute-done.3
  14.6 2.3 %collective-permute-start.4 = (bf16[256,256]{1,0:T(8,128)(2,1)S(1)}, bf16[256,256]{1,0:T(8,128)(2,1)S(1)}, u32[]{:S(2)}, u32[]{:S(2)}) collective-permute-start(bf16[256,256]{1,0:T(8,128)(2,1)S(1)} %fusion.7), channel_id=1, source_target_pairs={{0,4},{4,0},{1,5},{5,1},{2,6},{6,2},{3,7},{7,3},{8,12},{12,8},{9,1... | collective-permute-start | bytes 393224 | tf_op jit(solution)/shard_map/ppermute | solution.py:332
  16.8 0.7 fusion.23
  17.5 0.3 collective-permute-done.4
  17.8 0.1 fusion.6
  17.9 0.0 copy-done
  17.9 0.2 fusion.2
  18.1 0.0 copy-done.3
  18.1 0.2 fusion.3
  18.3 3.0 %collective-permute-start.5 = (bf16[256,256]{1,0:T(8,128)(2,1)S(1)}, bf16[256,256]{1,0:T(8,128)(2,1)S(1)}, u32[]{:S(2)}, u32[]{:S(2)}) collective-permute-start(bf16[256,256]{1,0:T(8,128)(2,1)S(1)} %pad_maximum_fusion.6.refs_3_), channel_id=1, source_target_pairs={{0,3},{1,0},{2,1},{3,2},{4,7},{5,4},{6,5},{7,6},{8,11},{9,8},{10,9... | collective-permute-start | bytes 393224 | tf_op jit(solution)/shard_map/ppermute | solution.py:332
  21.4 0.0 collective-permute-start.6
  21.4 0.2 convolution_add_fusion.1
  21.6 9.6 %collective-permute-done.5.refs_4_ = bf16[256,256]{1,0:T(8,128)(2,1)S(1)} collective-permute-done((bf16[256,256]{1,0:T(8,128)(2,1)S(1)}, bf16[256,256]{1,0:T(8,128)(2,1)S(1)}, u32[]{:S(2)}, u32[]{:S(2)}) %collective-permute-start.5) | collective-permute-done | bytes 131104 | tf_op jit(solution)/shard_map/ppermute | solution.py:332
  31.2 1.6 %collective-permute-done.6.refs_5_ = bf16[256,256]{1,0:T(8,128)(2,1)S(1)} collective-permute-done((bf16[256,256]{1,0:T(8,128)(2,1)S(1)}, bf16[256,256]{1,0:T(8,128)(2,1)S(1)}, u32[]{:S(2)}, u32[]{:S(2)}) %collective-permute-start.6) | collective-permute-done | bytes 131104 | tf_op jit(solution)/shard_map/ppermute | solution.py:332
  32.8 0.2 fusion.13
  33.0 0.2 fusion.20
  33.3 0.0 collective-permute-done.refs_1_
  33.3 0.4 convolution_add_fusion
  33.7 0.0 collective-permute-done.1.refs_2_
  33.7 0.3 convolution_add_fusion.2
  34.1 0.1 pad_maximum_fusion.1
  34.2 1.3 collective-permute-start.8
  35.5 1.3 collective-permute-done.8
  36.8 0.1 select_add_fusion
  36.9 22.9 %all_to_all.23 = f32[32,24,128]{2,1,0:T(8,128)} all-to-all(f32[32,24,128]{2,1,0:T(8,128)S(1)} %bitcast.34), channel_id=1, replica_groups=mesh['y'=4,'z'=8,'core'=2,'x'=4] {'y','z'}, dimensions={0} | all-to-all | bytes 786432 | tf_op jit(solution)/shard_map/all_to_all | solution.py:395
  59.8 1.0 reduce_sum.9
  60.9 13.0 %all_to_all.24 = f32[8,24,128]{2,1,0:T(8,128)S(1)} all-to-all(f32[8,24,128]{2,1,0:T(8,128)S(1)} %broadcast_in_dim.6), channel_id=1, replica_groups=mesh['y'=4,'z'=8,'core'=2,'x'=4] {'z'}, dimensions={0} | all-to-all | bytes 196608 | tf_op jit(solution)/shard_map/all_to_all | solution.py:340
  73.9 0.1 broadcast_in_dim.8
  74.1 22.0 %all_to_all.25 = f32[16,192,128]{2,1,0:T(8,128)S(1)} all-to-all(f32[16,192,128]{2,1,0:T(8,128)S(1)} %broadcast_in_dim.8), channel_id=1, replica_groups=mesh['y'=4,'z'=8,'core'=2,'x'=4] {'x','y'}, dimensions={0} | all-to-all | bytes 3145728 | tf_op jit(solution)/shard_map/all_to_all | solution.py:340
  96.0 0.0 copy-start.1
  96.0 4.7 %collective-permute-start.9 = (f32[3072,128]{1,0:T(8,128)S(1)}, f32[3072,128]{1,0:T(8,128)S(1)}, u32[]{:S(2)}, u32[]{:S(2)}) collective-permute-start(f32[3072,128]{1,0:T(8,128)S(1)} %bitcast.32), channel_id=1, source_target_pairs={{0,4},{4,0},{1,5},{5,1},{2,6},{6,2},{3,7},{7,3},{8,12},{12,8},{9,1... | collective-permute-start | bytes 4718600 | tf_op jit(solution)/shard_map/ppermute | solution.py:332
  100.7 0.1 pad_maximum_fusion
  100.8 1.1 collective-permute-start.7
  101.9 0.1 pad_add_fusion.where_ref
  102.0 1.8 %collective-permute-done.9.other_ref = f32[3072,128]{1,0:T(8,128)S(1)} collective-permute-done((f32[3072,128]{1,0:T(8,128)S(1)}, f32[3072,128]{1,0:T(8,128)S(1)}, u32[]{:S(2)}, u32[]{:S(2)}) %collective-permute-start.9) | collective-permute-done | bytes 1572896 | tf_op jit(solution)/shard_map/ppermute | solution.py:332
  103.8 0.0 copy-done.1
  103.8 49.6 %shard_map.64.refs_7_ = bf16[128,1024]{1,0:T(8,128)(2,1)S(1)} custom-call(s32[2]{0:T(128)S(1)} %pad_add_fusion.where_ref, f32[3072,128]{1,0:T(8,128)S(1)} %bitcast.33, f32[3072,128]{1,0:T(8,128)S(1)} %collective-permute-done.9.other_ref, f32[512,1024]{1,0:T(8,128)S(1)} %bitcast.31), custom_call_target="tpu_custom_call" | custom-call | flops 1000000 | bytes 1048576 | tf_op jit(solution)/shard_map/pallas_call | solution.py:259
  153.4 0.0 collective-permute-done.7.refs_6_
  153.4 2.2 %shard_map.65 = f32[2048,128]{1,0:T(8,128)} custom-call(bf16[1792,256]{1,0:T(8,128)(2,1)S(1)} %multiply_convert_fusion.refs_0_, bf16[1792,256]{1,0:T(8,128)(2,1)S(1)} %collective-permute-done.refs_1_, bf16[1792,256]{1,0:T(8,128)(2,1)S(1)} %collective-permute-done.1.refs_2_, bf16[256,256]{1,0:T(8,128)(2,1)S(1)} %pad_maximum_fusion.6.refs_3_, ...), custom_call_target="tpu_custom_call" | custom-call | tf_op jit(solution)/shard_map/pallas_call | solution.py:302
  (8 shorter events, 0.2 us)
Async XLA Ops:
  0.0 17.9 %copy-start = (f32[1,128,128]{2,1,0:T(8,128)S(1)}, f32[1,128,128]{2,1,0:T(8,128)}, u32[]{:S(2)}) copy-start(f32[1,128,128]{2,1,0:T(8,128)} %param.8) | copy-start | bytes 196612
  1.6 8.1 %copy-start.2 = (s32[1,2]{1,0:T(1,128)S(1)}, s32[1,2]{1,0:T(1,128)}, u32[]{:S(2)}) copy-start(s32[1,2]{1,0:T(1,128)} %param.10) | copy-start | bytes 28
  3.1 4.8 %collective-permute-start.2 = (bf16[128,256]{1,0:T(8,128)(2,1)S(1)}, bf16[128,256]{1,0:T(8,128)(2,1)S(1)}, u32[]{:S(2)}, u32[]{:S(2)}) collective-permute-start(bf16[128,256]{1,0:T(8,128)(2,1)S(1)} %broadcast_select_fusion.1), channel_id=1, source_target_pairs={{0,4},{4,0},{1,5},{5,1},{2,6},{6,2},{3,7},{7,3},{8,12},{12,8},{9,1... | collective-permute-start | bytes 196616 | tf_op jit(solution)/shard_map/ppermute | solution.py:332
  6.5 26.8 %collective-permute-start = (bf16[1792,256]{1,0:T(8,128)(2,1)S(1)}, bf16[1792,256]{1,0:T(8,128)(2,1)S(1)}, u32[]{:S(2)}, u32[]{:S(2)}) collective-permute-start(bf16[1792,256]{1,0:T(8,128)(2,1)S(1)} %multiply_convert_fusion.refs_0_), channel_id=1, source_target_pairs={{0,3},{1,0},{2,1},{3,2},{4,7},{5,4},{6,5},{7,6},{8,11},{9,8},{10,9... | collective-permute-start | bytes 2752520 | tf_op jit(solution)/shard_map/ppermute | solution.py:332
  7.2 26.5 %collective-permute-start.1 = (bf16[1792,256]{1,0:T(8,128)(2,1)S(1)}, bf16[1792,256]{1,0:T(8,128)(2,1)S(1)}, u32[]{:S(2)}, u32[]{:S(2)}) collective-permute-start(bf16[1792,256]{1,0:T(8,128)(2,1)S(1)} %multiply_convert_fusion.refs_0_), channel_id=1, source_target_pairs={{0,1},{1,2},{2,3},{3,0},{4,5},{5,6},{6,7},{7,4},{8,9},{9,10},{10,1... | collective-permute-start | bytes 2752520 | tf_op jit(solution)/shard_map/ppermute | solution.py:332
  8.0 6.5 %collective-permute-start.3 = (bf16[256,256]{1,0:T(8,128)(2,1)S(1)}, bf16[256,256]{1,0:T(8,128)(2,1)S(1)}, u32[]{:S(2)}, u32[]{:S(2)}) collective-permute-start(bf16[256,256]{1,0:T(8,128)(2,1)S(1)} %fusion.8), channel_id=1, source_target_pairs={{0,8},{8,16},{12,4},{16,24},{20,12},{24,32},{28,20},{32,40},{36,28... | collective-permute-start | bytes 393224 | tf_op jit(solution)/shard_map/ppermute | solution.py:322
  11.6 6.5 %copy-start.3 = (f32[1,128,128]{2,1,0:T(8,128)S(1)}, f32[1,128,128]{2,1,0:T(8,128)}, u32[]{:S(2)}) copy-start(f32[1,128,128]{2,1,0:T(8,128)} %param.9) | copy-start | bytes 196612
  14.6 3.2 %collective-permute-start.4 = (bf16[256,256]{1,0:T(8,128)(2,1)S(1)}, bf16[256,256]{1,0:T(8,128)(2,1)S(1)}, u32[]{:S(2)}, u32[]{:S(2)}) collective-permute-start(bf16[256,256]{1,0:T(8,128)(2,1)S(1)} %fusion.7), channel_id=1, source_target_pairs={{0,4},{4,0},{1,5},{5,1},{2,6},{6,2},{3,7},{7,3},{8,12},{12,8},{9,1... | collective-permute-start | bytes 393224 | tf_op jit(solution)/shard_map/ppermute | solution.py:332
  18.3 12.9 %collective-permute-start.5 = (bf16[256,256]{1,0:T(8,128)(2,1)S(1)}, bf16[256,256]{1,0:T(8,128)(2,1)S(1)}, u32[]{:S(2)}, u32[]{:S(2)}) collective-permute-start(bf16[256,256]{1,0:T(8,128)(2,1)S(1)} %pad_maximum_fusion.6.refs_3_), channel_id=1, source_target_pairs={{0,3},{1,0},{2,1},{3,2},{4,7},{5,4},{6,5},{7,6},{8,11},{9,8},{10,9... | collective-permute-start | bytes 393224 | tf_op jit(solution)/shard_map/ppermute | solution.py:332
  21.4 11.5 %collective-permute-start.6 = (bf16[256,256]{1,0:T(8,128)(2,1)S(1)}, bf16[256,256]{1,0:T(8,128)(2,1)S(1)}, u32[]{:S(2)}, u32[]{:S(2)}) collective-permute-start(bf16[256,256]{1,0:T(8,128)(2,1)S(1)} %pad_maximum_fusion.6.refs_3_), channel_id=1, source_target_pairs={{0,1},{1,2},{2,3},{3,0},{4,5},{5,6},{6,7},{7,4},{8,9},{9,10},{10,1... | collective-permute-start | bytes 393224 | tf_op jit(solution)/shard_map/ppermute | solution.py:332
  34.2 2.6 %collective-permute-start.8 = (f32[768,128]{1,0:T(8,128)S(1)}, f32[768,128]{1,0:T(8,128)S(1)}, u32[]{:S(2)}, u32[]{:S(2)}) collective-permute-start(f32[768,128]{1,0:T(8,128)S(1)} %slice_select_fusion), channel_id=1, source_target_pairs={{0,4},{4,0},{1,5},{5,1},{2,6},{6,2},{3,7},{7,3},{8,12},{12,8},{9,1... | collective-permute-start | bytes 1179656 | tf_op jit(solution)/shard_map/ppermute | solution.py:332
  96.0 7.7 %copy-start.1 = (f32[1024,512]{0,1:T(8,128)S(1)}, f32[1024,512]{0,1:T(8,128)}, u32[]{:S(2)}) copy-start(f32[1024,512]{0,1:T(8,128)} %copy.7) | copy-start | bytes 6291460
  96.0 7.7 %collective-permute-start.9 = (f32[3072,128]{1,0:T(8,128)S(1)}, f32[3072,128]{1,0:T(8,128)S(1)}, u32[]{:S(2)}, u32[]{:S(2)}) collective-permute-start(f32[3072,128]{1,0:T(8,128)S(1)} %bitcast.32), channel_id=1, source_target_pairs={{0,4},{4,0},{1,5},{5,1},{2,6},{6,2},{3,7},{7,3},{8,12},{12,8},{9,1... | collective-permute-start | bytes 4718600 | tf_op jit(solution)/shard_map/ppermute | solution.py:332
  100.8 52.6 %collective-permute-start.7 = (bf16[2048,256]{1,0:T(8,128)(2,1)S(1)}, bf16[2048,256]{1,0:T(8,128)(2,1)S(1)}, u32[]{:S(2)}, u32[]{:S(2)}) collective-permute-start(bf16[2048,256]{1,0:T(8,128)(2,1)S(1)} %pad_maximum_fusion), channel_id=1, source_target_pairs={{0,3},{1,0},{2,1},{3,2},{4,7},{5,4},{6,5},{7,6},{8,11},{9,8},{10,9... | collective-permute-start | bytes 3145736 | tf_op jit(solution)/shard_map/ppermute | solution.py:332
